TPU v7x, 128 devices: a whole 4x4x4 slice. The times are simulated.
128 devices in a mesh: row: 16 (over y, x), col: 8 (over z, core).
Axes of the slice: x: 4, y: 4, z: 4, core: 2. Of those that a mesh axis runs over, the one named last changes fastest.
Arguments:
- right_side: float32 [512, 32, 256], P(('row', 'col')), may hold values from -70 to 70
- diag_term: float32 [512, 256], P(('row', 'col')), may hold values from 2.5 to 8
- near_pairs: int32 [3, 8192], P(None, ('row', 'col')), may hold values from 0 to 511, as said below
- near_tiles: bfloat16 [8192, 256, 256], P(('row', 'col')), may hold values from -0.0390625 to 0.0390625
- far_pairs: int32 [3, 12288], P(None, ('row', 'col')), may hold values from 0 to 511, as said below
- far_factors: bfloat16 [12288, 2, 32, 256], P(('row', 'col')), may hold values from -0.0625 to 0.0625
Outputs:
- solution_field: float32 [512, 32, 256], P(('row', 'col'))
- residual: float32 [512, 32, 256], P(('row', 'col'))
Inputs may be any that keep to these rules, and one draw needn't show every extreme that they name: `near_pairs`: row 0 holds each slot's row cluster, row 1 its column cluster, row 2 a 1 for a live pair and 0 for an empty slot. The 64 slots of one device lie together in device order (row index slowest); its live slots come first, and some device has all 64 live. A slot's row cluster lies in the block of 32 clusters of its device's row index; its column cluster is no smaller, less than 4 clusters away, and before the end of the next block. `far_pairs`: row 0 holds each slot's row cluster, row 1 its column cluster, row 2 a 1 for a live pair and 0 for an empty slot. The 96 slots of one device lie together in device order (row index slowest); its live slots come first, and some device has all 96 live. A slot's row cluster lies in the block of 32 clusters of its device's row index; its column cluster is no smaller and lies before the end of the next block.
All inputs are finite; a program needn't handle non-finite values.
Results may differ from a plain program's by a relative error of at most 0.0033.
Values may be sent and summed in bfloat16 or wider, within the bound.
A program may use at most 64 MiB of HBM per device.

v0:
```python
import math

import jax
import jax.numpy as jnp
from jax import lax
from jax.sharding import PartitionSpec as P

ITERS = 3


def shifted(value, axis, steps):
    count = lax.axis_size(axis)
    leading, last = (max(0, -steps), min(count, count - steps))
    return lax.ppermute(value, axis, [(source, source + steps) for source in range(leading, last)])


def near_apply(from_col, from_row, tile_block):
    to_row = jnp.einsum("bnj,bij->bni", from_col, tile_block, preferred_element_type=jnp.float32)
    to_col = jnp.einsum("bni,bij->bnj", from_row, tile_block, preferred_element_type=jnp.float32)
    return (to_row, to_col)


def far_apply(from_col, from_row, factor_block):
    left_basis = factor_block[:, 0]
    right_basis = factor_block[:, 1]
    inner_part = jnp.einsum(
        "bnj,bkj->bnk", from_col, right_basis, preferred_element_type=jnp.float32
    ).astype(jnp.bfloat16)
    to_row = jnp.einsum("bnk,bki->bni", inner_part, left_basis, preferred_element_type=jnp.float32)
    outer_part = jnp.einsum(
        "bni,bki->bnk", from_row, left_basis, preferred_element_type=jnp.float32
    ).astype(jnp.bfloat16)
    to_col = jnp.einsum("bnk,bkj->bnj", outer_part, right_basis, preferred_element_type=jnp.float32)
    return (to_row, to_col)


def pair_sweep(summed, extended, pair_ids, stored, offset, apply_block):
    slot_count = pair_ids.shape[1]
    block_size = math.gcd(slot_count, 16)
    live_count = jnp.sum(pair_ids[2])
    turn_count = (live_count + block_size - 1) // block_size

    def one_turn(turn_index, acc):
        first_slot = turn_index * block_size
        chosen = lax.dynamic_slice_in_dim(pair_ids, first_slot, block_size, 1)
        stored_block = lax.dynamic_slice_in_dim(stored, first_slot, block_size, 0)
        row_ids = chosen[0] - offset
        col_ids = chosen[1] - offset
        weight = chosen[2].astype(jnp.float32)[:, None, None]
        to_row, to_col = apply_block(extended[col_ids], extended[row_ids], stored_block)
        return acc.at[row_ids].add(to_row * weight).at[col_ids].add(to_col * weight)

    return lax.fori_loop(jnp.int32(0), turn_count, one_turn, summed)


def body(right_side, diag_term, near_pairs, near_tiles, far_pairs, far_factors):
    own_count = right_side.shape[0]
    rhs_count = right_side.shape[1]
    panel_count = right_side.shape[2]
    group_size = own_count * lax.axis_size("col")
    offset = lax.axis_index("row") * group_size

    def residual_norm(field):
        return lax.psum(jnp.sum(field * field, axis=(0, 2)), ("row", "col"))

    solution_field = jnp.zeros_like(right_side)
    residual = right_side
    direction = right_side
    norm_now = residual_norm(residual)
    for iteration in range(ITERS):
        rounded = direction.astype(jnp.bfloat16)
        own_group = lax.all_gather(rounded, "col", axis=0, tiled=True)
        next_group = shifted(own_group, "row", -1)
        extended = jnp.concatenate([own_group, next_group], axis=0)
        summed = jnp.zeros((2 * group_size, rhs_count, panel_count), jnp.float32)
        summed = pair_sweep(summed, extended, near_pairs, near_tiles, offset, near_apply)
        summed = pair_sweep(summed, extended, far_pairs, far_factors, offset, far_apply)
        carried = shifted(summed[group_size:].astype(jnp.bfloat16), "row", 1).astype(jnp.float32)
        own_part = lax.psum_scatter(
            summed[:group_size] + carried, "col", scatter_dimension=0, tiled=True
        )
        image_field = diag_term[:, None, :] * direction + own_part
        curvature = lax.psum(jnp.sum(direction * image_field, axis=(0, 2)), ("row", "col"))
        step_size = norm_now / curvature
        solution_field = solution_field + step_size[None, :, None] * direction
        residual = residual - step_size[None, :, None] * image_field
        norm_next = residual_norm(residual)
        direction = residual + (norm_next / norm_now)[None, :, None] * direction
        norm_now = norm_next
    return (solution_field, residual)


def solution(mesh):
    placed = (
        P(("row", "col"), None, None),
        P(("row", "col"), None),
        P(None, ("row", "col")),
        P(("row", "col"), None, None),
        P(None, ("row", "col")),
        P(("row", "col"), None, None, None),
    )
    return jax.shard_map(
        body,
        mesh=mesh,
        in_specs=placed,
        out_specs=(P(("row", "col"), None, None), P(("row", "col"), None, None)),
        check_vma=False,
    )
```

profile of v0, /device:TPU:1, one launch (start us, length us, event | category | flops | bytes accessed | tf_op | source)
XLA Modules:
  0.0 1049.1 jit_solution(15026718704575420912)
XLA Ops:
  8.1 16.7 %all_gather.9 = bf16[32,32,256]{2,1,0:T(8,128)(2,1)} all-gather(bf16[4,32,256]{2,1,0:T(8,128)(2,1)S(1)} %convert_element_type.99), channel_id=1, replica_groups=mesh['row'=16,'col'=8] {'col'}, dimensions={0}, use_global_device_ids=true | all-gather | bytes 589824 | tf_op jit(solution)/shard_map/all_gather | solution.py:72
  34.3 6.1 collective-permute-done
  43.9 31.3 %while.60 = (s32[]{:T(128)}, f32[64,32,256]{2,1,0:T(8,128)}, s32[]{:T(128)}, s32[3,64]{1,0:T(4,128)S(1)}, s32[]{:T(128)}, /*index=5*/bf16[64,32,256]{2,1,0:T(8,1...) while((s32[]{:T(128)}, f32[64,32,256]{2,1,0:T(8,128)}, ...), condition=%wide.region_6.7_spmd, body=%wide.region_3.6_spmd.sunk | while | flops 134744224 | bytes 9971115 | solution.py:53
  45.8 3.1 fusion.109
  48.9 3.0 scatter_fusion
  61.5 3.1 fusion.109
  64.6 3.0 scatter_fusion
  75.3 23.9 %while.61 = (s32[]{:T(128)}, f32[64,32,256]{2,1,0:T(8,128)}, s32[]{:T(128)}, s32[3,96]{1,0:T(4,128)S(1)}, s32[]{:T(128)}, /*index=5*/bf16[64,32,256]{2,1,0:T(8,1...) while((s32[]{:T(128)}, f32[64,32,256]{2,1,0:T(8,128)}, ...), condition=%wide.region_11.12_spmd, body=%wide.region_8.11_spmd.sunk | while | flops 34113688 | bytes 6829367 | solution.py:53
  100.5 46.5 %collective-permute-start.1 = (bf16[32,32,256]{2,1,0:T(8,128)(2,1)S(1)}, bf16[32,32,256]{2,1,0:T(8,128)(2,1)S(1)}, u32[]{:S(2)}, u32[]{:S(2)}) collective-permute-start(bf16[32,32,256]{2,1,0:T(8,128)(2,1)S(1)} %slice.166), channel_id=1, source_target_pairs={{0,8},{8,16},{16,24},{24,32},{32,40},{40,48},{48,56},{56,64},{64,7... | collective-permute-start | bytes 1572872 | tf_op jit(solution)/shard_map/ppermute | solution.py:14
  147.0 6.1 collective-permute-done.1
  155.6 68.8 %reduce-scatter.4.cloned.1.call-done = f32[4,32,256]{2,1,0:T(8,128)} async-done(((f32[32,32,256]{2,1,0:T(8,128)}), f32[4,32,256]{2,1,0:T(8,128)}) %reduce-scatter.4.cloned.1.call-update) | async-done | bytes 131088 | tf_op jit(solution)/shard_map/reduce_scatter | solution.py:79
  225.4 67.5 %all-reduce = (f32[32]{0:T(128)S(1)}, f32[32]{0:T(128)S(1)}) all-reduce(f32[32]{0:T(128)S(1)} %get-tuple-element.279, f32[32]{0:T(128)S(1)} %get-tuple-element.278), channel_id=1, replica_groups=mesh['row'=16,'col'=8] {'row','col'}, use_global_device_ids=true, to_apply=%region_1.0 | all-reduce | flops 64 | bytes 512 | tf_op jit(solution)/shard_map/psum | solution.py:64
  294.1 62.5 %psum.44 = f32[32]{0:T(128)S(1)} all-reduce(f32[32]{0:T(128)S(1)} %multiply_reduce_fusion.3), channel_id=1, replica_groups=mesh['row'=16,'col'=8] {'row','col'}, use_global_device_ids=true, to_apply=%region_16.17 | all-reduce | flops 32 | bytes 256 | tf_op jit(solution)/shard_map/psum | solution.py:64
  358.1 14.6 %all_gather.10 = bf16[32,32,256]{2,1,0:T(8,128)(2,1)} all-gather(bf16[4,32,256]{2,1,0:T(8,128)(2,1)S(1)} %get-tuple-element.368), channel_id=1, replica_groups=mesh['row'=16,'col'=8] {'col'}, dimensions={0}, use_global_device_ids=true | all-gather | bytes 589824 | tf_op jit(solution)/shard_map/all_gather | solution.py:72
  375.9 12.4 %collective-permute-done.2 = bf16[32,32,256]{2,1,0:T(8,128)(2,1)} collective-permute-done((bf16[32,32,256]{2,1,0:T(8,128)(2,1)}, bf16[32,32,256]{2,1,0:T(8,128)(2,1)}, u32[]{:S(2)}, u32[]{:S(2)}) %collective-permute-start.2) | collective-permute-done | bytes 524320 | tf_op jit(solution)/shard_map/ppermute | solution.py:14
  391.8 34.7 %while.62 = (s32[]{:T(128)}, f32[64,32,256]{2,1,0:T(8,128)}, s32[]{:T(128)}, s32[3,64]{1,0:T(4,128)S(1)}, s32[]{:T(128)}, /*index=5*/bf16[64,32,256]{2,1,0:T(8,1...) while((s32[]{:T(128)}, f32[64,32,256]{2,1,0:T(8,128)}, ...), condition=%wide.region_20.21_spmd, body=%wide.region_17.0_spmd.sunk | while | flops 134744224 | bytes 9973211 | solution.py:53
  395.1 3.1 fusion.119
  398.2 3.1 scatter_fusion.4
  406.0 3.1 scatter_fusion.5
  412.5 3.1 fusion.119
  415.6 3.1 scatter_fusion.4
  423.3 3.1 scatter_fusion.5
  426.5 30.8 %while.63 = (s32[]{:T(128)}, f32[64,32,256]{2,1,0:T(8,128)}, s32[]{:T(128)}, s32[3,96]{1,0:T(4,128)S(1)}, s32[]{:T(128)}, /*index=5*/bf16[64,32,256]{2,1,0:T(8,1...) while((s32[]{:T(128)}, f32[64,32,256]{2,1,0:T(8,128)}, ...), condition=%wide.region_24.25_spmd, body=%wide.region_21.0_spmd.sunk | while | flops 34113688 | bytes 6829835 | solution.py:53
  432.1 3.1 scatter_fusion.6
  438.8 3.1 scatter_fusion.7
  447.5 3.1 scatter_fusion.6
  454.2 3.1 scatter_fusion.7
  458.6 53.2 %collective-permute-start.3 = (bf16[32,32,256]{2,1,0:T(8,128)(2,1)S(1)}, bf16[32,32,256]{2,1,0:T(8,128)(2,1)S(1)}, u32[]{:S(2)}, u32[]{:S(2)}) collective-permute-start(bf16[32,32,256]{2,1,0:T(8,128)(2,1)S(1)} %slice.165), channel_id=1, source_target_pairs={{0,8},{8,16},{16,24},{24,32},{32,40},{40,48},{48,56},{56,64},{64,7... | collective-permute-start | bytes 1572872 | tf_op jit(solution)/shard_map/ppermute | solution.py:14
  511.9 6.1 collective-permute-done.3
  520.4 77.2 %reduce-scatter.6.cloned.1.call-done = f32[4,32,256]{2,1,0:T(8,128)} async-done(((f32[32,32,256]{2,1,0:T(8,128)}), f32[4,32,256]{2,1,0:T(8,128)}) %reduce-scatter.6.cloned.1.call-update) | async-done | bytes 131088 | tf_op jit(solution)/shard_map/reduce_scatter | solution.py:79
  599.2 67.5 %psum.45 = f32[32]{0:T(128)} all-reduce(f32[32]{0:T(128)} %multiply_reduce_fusion.2), channel_id=1, replica_groups=mesh['row'=16,'col'=8] {'row','col'}, use_global_device_ids=true, to_apply=%region_27.28 | all-reduce | flops 32 | bytes 256 | tf_op jit(solution)/shard_map/psum | solution.py:83
  669.6 62.6 %psum.46 = f32[32]{0:T(128)S(1)} all-reduce(f32[32]{0:T(128)} %get-tuple-element.366), channel_id=1, replica_groups=mesh['row'=16,'col'=8] {'row','col'}, use_global_device_ids=true, to_apply=%region_29.30 | all-reduce | flops 32 | bytes 256 | tf_op jit(solution)/shard_map/psum | solution.py:64
  733.8 14.6 %all_gather.11 = bf16[32,32,256]{2,1,0:T(8,128)(2,1)} all-gather(bf16[4,32,256]{2,1,0:T(8,128)(2,1)S(1)} %fusion.60), channel_id=1, replica_groups=mesh['row'=16,'col'=8] {'col'}, dimensions={0}, use_global_device_ids=true | all-gather | bytes 589824 | tf_op jit(solution)/shard_map/all_gather | solution.py:72
  751.6 12.4 %collective-permute-done.4 = bf16[32,32,256]{2,1,0:T(8,128)(2,1)} collective-permute-done((bf16[32,32,256]{2,1,0:T(8,128)(2,1)}, bf16[32,32,256]{2,1,0:T(8,128)(2,1)}, u32[]{:S(2)}, u32[]{:S(2)}) %collective-permute-start.4) | collective-permute-done | bytes 524320 | tf_op jit(solution)/shard_map/ppermute | solution.py:14
  767.5 34.6 %while.64 = (s32[]{:T(128)}, f32[64,32,256]{2,1,0:T(8,128)}, s32[]{:T(128)}, s32[3,64]{1,0:T(4,128)S(1)}, s32[]{:T(128)}, /*index=5*/bf16[64,32,256]{2,1,0:T(8,1...) while((s32[]{:T(128)}, f32[64,32,256]{2,1,0:T(8,128)}, ...), condition=%wide.region_33.34_spmd, body=%wide.region_30.0_spmd.sunk | while | flops 134744224 | bytes 9973211 | solution.py:53
  770.8 3.1 fusion.129
  773.9 3.1 scatter_fusion.8
  781.7 3.1 scatter_fusion.9
  788.1 3.1 fusion.129
  791.2 3.1 scatter_fusion.8
  799.0 3.1 scatter_fusion.9
  802.1 30.5 %while.65 = (s32[]{:T(128)}, f32[64,32,256]{2,1,0:T(8,128)}, s32[]{:T(128)}, s32[3,96]{1,0:T(4,128)S(1)}, s32[]{:T(128)}, /*index=5*/bf16[64,32,256]{2,1,0:T(8,1...) while((s32[]{:T(128)}, f32[64,32,256]{2,1,0:T(8,128)}, ...), condition=%wide.region_37.38_spmd, body=%wide.region_34.37_spmd.sunk | while | flops 34113688 | bytes 6830119 | solution.py:53
  807.6 3.1 scatter_fusion.10
  822.9 3.1 scatter_fusion.10
  834.0 53.0 %collective-permute-start.5 = (bf16[32,32,256]{2,1,0:T(8,128)(2,1)S(1)}, bf16[32,32,256]{2,1,0:T(8,128)(2,1)S(1)}, u32[]{:S(2)}, u32[]{:S(2)}) collective-permute-start(bf16[32,32,256]{2,1,0:T(8,128)(2,1)S(1)} %slice.164), channel_id=1, source_target_pairs={{0,8},{8,16},{16,24},{24,32},{32,40},{40,48},{48,56},{56,64},{64,7... | collective-permute-start | bytes 1572872 | tf_op jit(solution)/shard_map/ppermute | solution.py:14
  887.0 6.1 collective-permute-done.5
  895.5 76.7 %reduce-scatter.8.cloned.1.call-done = f32[4,32,256]{2,1,0:T(8,128)} async-done(((f32[32,32,256]{2,1,0:T(8,128)}), f32[4,32,256]{2,1,0:T(8,128)}) %reduce-scatter.8.cloned.1.call-update) | async-done | bytes 131088 | tf_op jit(solution)/shard_map/reduce_scatter | solution.py:79
  973.3 67.5 %psum.47 = f32[32]{0:T(128)S(1)} all-reduce(f32[32]{0:T(128)S(1)} %multiply_reduce_fusion), channel_id=1, replica_groups=mesh['row'=16,'col'=8] {'row','col'}, use_global_device_ids=true, to_apply=%region_40.41 | all-reduce | flops 32 | bytes 256 | tf_op jit(solution)/shard_map/psum | solution.py:83
  (235 shorter events, 166.8 us)
Async XLA Ops:
  7.2 217.2 %reduce-scatter.4.cloned.1.call-start = ((), (), s32[]{:S(2)}) async-start(), calls=%async_computation.3 | async-start | bytes 1179648 | tf_op jit(solution)/shard_map/reduce_scatter | solution.py:79
  24.9 15.6 %collective-permute-start = (bf16[32,32,256]{2,1,0:T(8,128)(2,1)}, bf16[32,32,256]{2,1,0:T(8,128)(2,1)}, u32[]{:S(2)}, u32[]{:S(2)}) collective-permute-start(bf16[32,32,256]{2,1,0:T(8,128)(2,1)} %all_gather.9), channel_id=1, source_target_pairs={{8,0},{16,8},{24,16},{32,24},{40,32},{48,40},{56,48},{64,56},{72,6... | collective-permute-start | bytes 1572872 | tf_op jit(solution)/shard_map/ppermute | solution.py:14
  32.4 11.5 %copy-start.5 = (s32[3,64]{1,0:T(4,128)S(1)}, s32[3,64]{1,0:T(4,128)}, u32[]{:S(2)}) copy-start(s32[3,64]{1,0:T(4,128)} %param.20) | copy-start | bytes 2308
  43.9 31.4 %copy-start.6 = (s32[3,96]{1,0:T(4,128)S(1)}, s32[3,96]{1,0:T(4,128)}, u32[]{:S(2)}) copy-start(s32[3,96]{1,0:T(4,128)} %param.22) | copy-start | bytes 3460
  100.5 123.9 %copy-start = (f32[4,32,256]{2,1,0:T(8,128)S(1)}, f32[4,32,256]{2,1,0:T(8,128)}, u32[]{:S(2)}) copy-start(f32[4,32,256]{2,1,0:T(8,128)} %param.18) | copy-start | bytes 393220
  100.5 123.9 %copy-start.7 = (f32[4,256]{1,0:T(4,128)S(1)}, f32[4,256]{1,0:T(4,128)}, u32[]{:S(2)}) copy-start(f32[4,256]{1,0:T(4,128)} %param.19) | copy-start | bytes 12292
  100.5 52.6 %collective-permute-start.1 = (bf16[32,32,256]{2,1,0:T(8,128)(2,1)S(1)}, bf16[32,32,256]{2,1,0:T(8,128)(2,1)S(1)}, u32[]{:S(2)}, u32[]{:S(2)}) collective-permute-start(bf16[32,32,256]{2,1,0:T(8,128)(2,1)S(1)} %slice.166), channel_id=1, source_target_pairs={{0,8},{8,16},{16,24},{24,32},{32,40},{40,48},{48,56},{56,64},{64,7... | collective-permute-start | bytes 1572872 | tf_op jit(solution)/shard_map/ppermute | solution.py:14
  155.5 442.1 %reduce-scatter.6.cloned.1.call-start = ((), (), s32[]{:S(2)}) async-start(), calls=%async_computation.4 | async-start | bytes 1179648 | tf_op jit(solution)/shard_map/reduce_scatter | solution.py:79
  292.9 98.9 %copy-start.23 = (f32[32]{0:T(128)}, f32[32]{0:T(128)S(1)}, u32[]{:S(2)}) copy-start(f32[32]{0:T(128)S(1)} %div.40) | copy-start | bytes 388
  372.7 15.6 %collective-permute-start.2 = (bf16[32,32,256]{2,1,0:T(8,128)(2,1)}, bf16[32,32,256]{2,1,0:T(8,128)(2,1)}, u32[]{:S(2)}, u32[]{:S(2)}) collective-permute-start(bf16[32,32,256]{2,1,0:T(8,128)(2,1)} %all_gather.10), channel_id=1, source_target_pairs={{8,0},{16,8},{24,16},{32,24},{40,32},{48,40},{56,48},{64,56},{72,6... | collective-permute-start | bytes 1572872 | tf_op jit(solution)/shard_map/ppermute | solution.py:14
  391.9 0.6 copy-start.17
  391.9 0.6 copy-start.11
  391.9 0.6 copy-start.15
  395.1 3.1 copy-start.21
  409.2 0.6 copy-start.17
  409.2 0.6 copy-start.11
  409.2 0.6 copy-start.15
  412.5 3.1 copy-start.21
  426.6 0.6 copy-start.18
  426.6 0.6 copy-start.8
  426.6 0.6 copy-start.13
  442.0 0.6 copy-start.18
  442.0 0.6 copy-start.8
  442.0 0.6 copy-start.13
  458.6 208.7 %copy-start.1 = (f32[4,32,256]{2,1,0:T(8,128)S(1)}, f32[4,32,256]{2,1,0:T(8,128)}, u32[]{:S(2)}) copy-start(f32[4,32,256]{2,1,0:T(8,128)} %param.18) | copy-start | bytes 393220
  458.6 208.7 %copy-start.3 = (f32[4,32,256]{2,1,0:T(8,128)S(1)}, f32[4,32,256]{2,1,0:T(8,128)}, u32[]{:S(2)}) copy-start(f32[4,32,256]{2,1,0:T(8,128)} %reduce-scatter.4.cloned.1.call-done) | copy-start | bytes 393220
  458.6 208.7 %copy-start.24 = (f32[32]{0:T(128)S(1)}, f32[32]{0:T(128)}, u32[]{:S(2)}) copy-start(f32[32]{0:T(128)} %copy-done.23) | copy-start | bytes 388
  458.6 59.3 %collective-permute-start.3 = (bf16[32,32,256]{2,1,0:T(8,128)(2,1)S(1)}, bf16[32,32,256]{2,1,0:T(8,128)(2,1)S(1)}, u32[]{:S(2)}, u32[]{:S(2)}) collective-permute-start(bf16[32,32,256]{2,1,0:T(8,128)(2,1)S(1)} %slice.165), channel_id=1, source_target_pairs={{0,8},{8,16},{16,24},{24,32},{32,40},{40,48},{48,56},{56,64},{64,7... | collective-permute-start | bytes 1572872 | tf_op jit(solution)/shard_map/ppermute | solution.py:14
  520.4 451.8 %reduce-scatter.8.cloned.1.call-start = ((), (), s32[]{:S(2)}) async-start(), calls=%async_computation.5 | async-start | bytes 1179648 | tf_op jit(solution)/shard_map/reduce_scatter | solution.py:79
  667.3 2.3 copy-start.28
  732.2 35.3 %copy-start.31 = (f32[32]{0:T(128)}, f32[32]{0:T(128)S(1)}, u32[]{:S(2)}) copy-start(f32[32]{0:T(128)S(1)} %psum.46) | copy-start | bytes 388
  732.8 15.6 %copy-start.26 = (f32[32]{0:T(128)}, f32[32]{0:T(128)S(1)}, u32[]{:S(2)}) copy-start(f32[32]{0:T(128)S(1)} %div.43) | copy-start | bytes 388
  748.4 15.6 %collective-permute-start.4 = (bf16[32,32,256]{2,1,0:T(8,128)(2,1)}, bf16[32,32,256]{2,1,0:T(8,128)(2,1)}, u32[]{:S(2)}, u32[]{:S(2)}) collective-permute-start(bf16[32,32,256]{2,1,0:T(8,128)(2,1)} %all_gather.11), channel_id=1, source_target_pairs={{8,0},{16,8},{24,16},{32,24},{40,32},{48,40},{56,48},{64,56},{72,6... | collective-permute-start | bytes 1572872 | tf_op jit(solution)/shard_map/ppermute | solution.py:14
  767.6 0.6 copy-start.19
  767.6 0.6 copy-start.12
  770.8 3.1 copy-start.22
  784.9 0.6 copy-start.19
  784.9 0.6 copy-start.12
  788.1 3.1 copy-start.22
  805.8 8.5 copy-start.10
  821.1 8.5 copy-start.10
  833.9 138.3 %copy-start.4 = (f32[4,32,256]{2,1,0:T(8,128)S(1)}, f32[4,32,256]{2,1,0:T(8,128)}, u32[]{:S(2)}) copy-start(f32[4,32,256]{2,1,0:T(8,128)} %get-tuple-element.367) | copy-start | bytes 393220
  833.9 138.3 %copy-start.27 = (f32[32]{0:T(128)S(1)}, f32[32]{0:T(128)}, u32[]{:S(2)}) copy-start(f32[32]{0:T(128)} %copy-done.26) | copy-start | bytes 388
  833.9 206.9 %copy-start.32 = (f32[32]{0:T(128)S(1)}, f32[32]{0:T(128)}, u32[]{:S(2)}) copy-start(f32[32]{0:T(128)} %copy-done.31) | copy-start | bytes 388
  833.9 206.9 %copy-start.2 = (f32[4,32,256]{2,1,0:T(8,128)S(1)}, f32[4,32,256]{2,1,0:T(8,128)}, u32[]{:S(2)}) copy-start(f32[4,32,256]{2,1,0:T(8,128)} %param.18) | copy-start | bytes 393220
  833.9 206.9 %copy-start.25 = (f32[32]{0:T(128)S(1)}, f32[32]{0:T(128)}, u32[]{:S(2)}) copy-start(f32[32]{0:T(128)} %copy-done.23) | copy-start | bytes 388
  833.9 206.9 %copy-start.29 = (f32[32]{0:T(128)S(1)}, f32[32]{0:T(128)}, u32[]{:S(2)}) copy-start(f32[32]{0:T(128)} %copy-done.28) | copy-start | bytes 388
  834.0 59.1 %collective-permute-start.5 = (bf16[32,32,256]{2,1,0:T(8,128)(2,1)S(1)}, bf16[32,32,256]{2,1,0:T(8,128)(2,1)S(1)}, u32[]{:S(2)}, u32[]{:S(2)}) collective-permute-start(bf16[32,32,256]{2,1,0:T(8,128)(2,1)S(1)} %slice.164), channel_id=1, source_target_pairs={{0,8},{8,16},{16,24},{24,32},{32,40},{40,48},{48,56},{56,64},{64,7... | collective-permute-start | bytes 1572872 | tf_op jit(solution)/shard_map/ppermute | solution.py:14
  (9 other events, 5.3 us)
Sparse Core Ops, SparseCore 0:
  155.6 68.6 reduce-scatter.3
  520.5 77.0 reduce-scatter.5
  895.6 76.5 reduce-scatter.7
where the time goes:
time: 1060 us; the launch traced here: 1050 us
  blocking collectives  374 us (35%)
  waiting for transfers between devices  272 us (26%)
  starting transfers between devices  157 us (15%)
  other arithmetic  108 us (10%)
  local copies, waits for them, and re-layouts  68.6 us (6%)
  matrix products  54.6 us (5%)
  between operations  15.4 us (1%)
    reduce_scatter x3, waiting for transfers between devices, body(): lax.psum_scatter(summed[:group_size] + carried, 'col', scatter_dimension=...  223 us
    psum x3, blocking collectives, residual_norm(): return lax.psum(jnp.sum(field * field, axis=(0, 2)), ('row', 'col'))  193 us
    ppermute x6, starting transfers between devices, shifted(): lax.ppermute(value, axis, [(source, source + steps) for source in range(l...  157 us
    psum x2, blocking collectives, body(): lax.psum(jnp.sum(direction * image_field, axis=(0, 2)), ('row', 'col'))  135 us
    scatter-add x24, other arithmetic, one_turn(): return acc.at[row_ids].add(to_row * weight).at[col_ids].add(to_col * weight)  73.8 us
    ppermute x6, waiting for transfers between devices, shifted(): lax.ppermute(value, axis, [(source, source + steps) for source in range(l...  49.1 us
    all_gather x3, blocking collectives, body(): own_group = lax.all_gather(rounded, 'col', axis=0, tiled=True)  45.9 us
    gather x12, local copies, waits for them, and re-layouts, one_turn(): extended[col_ids]  22.2 us
  transfers between devices with their start and end apart: 9, of which 9 were waited for; matrix products, arithmetic and copies ran while one was open for 1% of the time, Pallas kernels for 0%

commit v1 on v0

v1 whole, which is shorter than its diff:
```python
import functools

import jax
import jax.numpy as jnp
from jax import lax
from jax.experimental import pallas as pl
from jax.experimental.pallas import tpu as pltpu
from jax.sharding import PartitionSpec as P

ITERS = 3
MESH = pl.DeviceIdType.MESH
NEAR_UNROLL = 16
FAR_UNROLL = 6
F32 = jnp.float32
BF16 = jnp.bfloat16

XO_Z = 0
XO_SIB = 3
XN_ROW = 7
XN_SIB = 11
PR_NEXT = 15
PR_OWN = 16
RN = 17
RO = 21
AR_COL = 24
AR_ROW = 31
N_SEM = 46


def sorted_tables(key, source, dummy):
    count = key.shape[0]
    ids = jnp.arange(count, dtype=jnp.int32)
    before = (key[None, :] < key[:, None]) | ((key[None, :] == key[:, None]) & (ids[None, :] < ids[:, None]))
    rank = jnp.sum(before.astype(jnp.int32), axis=1)
    hit = (rank[:, None] == ids[None, :]).astype(jnp.int32)
    slot = jnp.sum(hit * ids[:, None], axis=0)
    src = jnp.sum(hit * source[:, None], axis=0)
    skey = jnp.sum(hit * key[:, None], axis=0)
    places = jnp.arange(64, dtype=jnp.int32)
    upto = jnp.sum((key[:, None] <= places[None, :]).astype(jnp.int32), axis=0)
    equal = jnp.sum((key[:, None] == places[None, :]).astype(jnp.int32), axis=0)
    last = jnp.where(equal > 0, upto - 1, dummy)
    pad = lambda v: jnp.pad(v, (0, 128 - v.shape[0]))
    return [pad(slot), pad(src), pad(skey), pad(last)]


def make_tables(near_pairs, far_pairs, offset):
    rows = []
    for pairs in (near_pairs, far_pairs):
        count = pairs.shape[1]
        row = jnp.clip(pairs[0] - offset, 0, 31)
        col = jnp.clip(pairs[1] - offset, 0, 63)
        live = pairs[2] != 0
        rows += sorted_tables(jnp.where(live, col, 64), row, count)
        rows += sorted_tables(jnp.where(live, row, 64), col, count)
    return jnp.stack(rows)


def kernel(
    tab, b_ref, diag_ref, tiles_hbm, fac_hbm, x_ref, r_ref,
    tiles, fac, pn, pf, xo, xn, ext, acc1, stn, sto, prn, pro, zsn, zso, rn, ro, ar1, ar2,
    p_ref, q_ref, gd, sc, ss, rs, ls,
):
    g = lax.axis_index("row")
    me = lax.axis_index("col")
    n_row = lax.axis_size("row")
    n_col = lax.axis_size("col")
    z, core = me // 2, me % 2
    n_z = n_col // 2
    sib = z * 2 + (1 - core)
    nxt, prv = (g + 1) % n_row, (g + n_row - 1) % n_row
    k_near = tiles.shape[0]
    k_far = fac.shape[0]

    def zc(d):
        return ((z + d + n_z) % n_z) * 2 + core

    def zs(d):
        return ((z + d + n_z) % n_z) * 2 + (1 - core)

    def rdma(it, idx, src, dst, row, col):
        return pltpu.make_async_remote_copy(
            src_ref=src, dst_ref=dst, send_sem=ss.at[it, idx], recv_sem=rs.at[it, idx],
            device_id=(row, col), device_id_type=MESH,
        )

    def shard(ref, it, col):
        return ref.at[it, pl.ds(col * 4, 4)]

    load_tiles = pltpu.make_async_copy(tiles_hbm, tiles, ls.at[0])
    load_fac = pltpu.make_async_copy(fac_hbm, fac, ls.at[1])
    load_tiles.start()
    load_fac.start()

    barrier = pltpu.get_barrier_semaphore()
    peers = [(g, (me + k) % n_col) for k in range(1, n_col)]
    peers += [((g + k) % n_row, me) for k in range(1, n_row)]
    peers += [(nxt, zc(d)) for d in range(1, n_z)] + [(prv, zc(d)) for d in range(1, n_z)]
    for peer in peers:
        pl.semaphore_signal(barrier, inc=1, device_id=peer, device_id_type=MESH)

    sub = lax.broadcasted_iota(jnp.int32, (32, 128), 0)
    lane = lax.broadcasted_iota(jnp.int32, (32, 128), 1)

    def lane_sum(field):
        return jnp.sum(field[:, :128] + field[:, 128:], axis=1, keepdims=True)

    def to_row(cols):
        total = jnp.zeros((32, 128), F32)
        for j, col in enumerate(cols):
            total += jnp.where(lane == sub + 32 * j, col, 0.0)
        return jnp.sum(total, axis=0, keepdims=True)

    def to_col(row, j):
        return jnp.sum(jnp.where(lane == sub + 32 * j, row, 0.0), axis=1, keepdims=True)

    def wide(col):
        return jnp.broadcast_to(col, (32, 128))

    total = jnp.zeros((32, 256), F32)
    for j in range(4):
        r = b_ref[j]
        r_ref[j] = r
        x_ref[j] = jnp.zeros((32, 256), F32)
        p_ref[j] = jnp.zeros((32, 256), F32)
        q_ref[j] = jnp.zeros((32, 256), F32)
        xo[0, me * 4 + j] = r.astype(BF16)
        total += r * r
    gd[0] = wide(lane_sum(total))
    gd[1] = jnp.zeros((32, 128), F32)
    sc[0] = jnp.ones((32, 128), F32)
    sc[1] = jnp.zeros((32, 128), F32)
    pn[k_near] = jnp.zeros((32, 256), F32)
    pf[k_far] = jnp.zeros((32, 256), F32)

    pl.semaphore_wait(barrier, len(peers))

    def first_sends(it):
        mine = shard(xo, it, me)
        return [
            rdma(it, XO_Z + d - 1, mine, mine, g, zc(d)) for d in (1, 3, 2)
        ] + [
            rdma(it, XO_SIB, mine, mine, g, sib),
            rdma(it, XN_ROW, mine, shard(xn, it, me), prv, me),
        ]

    def from_z(it, d):
        here = shard(xo, it, zc(-d))
        return rdma(it, XO_Z + d - 1, here, here, g, zc(d))

    def relays(it, d):
        here = shard(xo, it, zc(-d))
        return [
            rdma(it, XO_SIB + d, here, here, g, sib),
            rdma(it, XN_ROW + d, here, shard(xn, it, zc(-d)), prv, me),
        ]

    def from_sib(it, d):
        here = shard(xo, it, zs(-d))
        return rdma(it, XO_SIB + d, here, here, g, sib)

    def next_from_row(it, d):
        here = shard(xn, it, zc(-d))
        return rdma(it, XN_ROW + d, here, here, prv, me)

    def next_to_sib(it, d):
        here = shard(xn, it, zc(-d))
        return rdma(it, XN_SIB + d, here, here, g, sib)

    def next_from_sib(it, d):
        here = shard(xn, it, zs(-d))
        return rdma(it, XN_SIB + d, here, here, g, sib)

    def pair_next(it):
        return rdma(it, PR_NEXT, stn.at[it, 1 - core], prn.at[it], g, sib)

    def pair_own(it):
        return rdma(it, PR_OWN, sto.at[it, 1 - core], pro.at[it], g, sib)

    def terms_next(it, d):
        return rdma(it, RN + d, zsn.at[it, (z + d) % n_z], rn.at[it, d], nxt, zc(d))

    def terms_own(it, d):
        return rdma(it, RO + d - 1, zso.at[it, (z + d) % n_z], ro.at[it, d - 1], g, zc(d))

    def dots_col(it, k):
        return rdma(it, AR_COL + k - 1, ar1.at[it, me], ar1.at[it, me], g, (me + k) % n_col)

    def dots_col_in(it, k):
        here = ar1.at[it, (me + n_col - k) % n_col]
        return rdma(it, AR_COL + k - 1, here, here, g, (me + k) % n_col)

    def dots_row(it, k):
        return rdma(it, AR_ROW + k - 1, ar2.at[it, g], ar2.at[it, g], (g + k) % n_row, me)

    def dots_row_in(it, k):
        here = ar2.at[it, (g + n_row - k) % n_row]
        return rdma(it, AR_ROW + k - 1, here, here, (g + k) % n_row, me)

    def near_phase(base, transposed):
        def step(block, acc):
            for u in range(NEAR_UNROLL):
                k = block * NEAR_UNROLL + u
                field = ext[tab[base + 1, k]]
                tile = tiles[tab[base, k]]
                keep = (tab[base + 2, k] == tab[base + 2, lax.max(k - 1, 0)]).astype(F32)
                term = lax.dot_general(
                    field, tile, (((1,), (1 if transposed else 0,)), ((), ())),
                    preferred_element_type=F32,
                )
                acc = acc * keep + term
                pn[k] = acc
            return acc

        lax.fori_loop(0, k_near // NEAR_UNROLL, step, jnp.zeros((32, 256), F32))

    def far_phase(base, first, second):
        lanes = lax.broadcasted_iota(jnp.int32, (256, 256), 1) // 32
        rows = lax.broadcasted_iota(jnp.int32, (256, 256), 0) // 32
        mask = lanes == rows

        def step(block, acc):
            for u in range(FAR_UNROLL):
                start = (block * FAR_UNROLL + u) * 8
                fields, lefts, rights = [], [], []
                for q in range(8):
                    slot = tab[base, start + q]
                    fields.append(ext[tab[base + 1, start + q]])
                    lefts.append(fac[slot, first])
                    rights.append(fac[slot, second])
                field = jnp.concatenate(fields, axis=0)
                left = jnp.concatenate(lefts, axis=0)
                right = jnp.concatenate(rights, axis=0)
                inner = lax.dot_general(field, left, (((1,), (1,)), ((), ())), preferred_element_type=F32)
                inner = jnp.where(mask, inner, 0.0).astype(BF16)
                term = lax.dot_general(inner, right, (((1,), (0,)), ((), ())), preferred_element_type=F32)
                for q in range(8):
                    k = start + q
                    keep = (tab[base + 2, k] == tab[base + 2, lax.max(k - 1, 0)]).astype(F32)
                    acc = acc * keep + term[q * 32 : q * 32 + 32]
                    pf[k] = acc
            return acc

        lax.fori_loop(0, k_far // (8 * FAR_UNROLL), step, jnp.zeros((32, 256), F32))

    for copy in first_sends(0):
        copy.start()
    load_tiles.wait()
    load_fac.wait()

    def iteration(it, carry):
        for d in (1, 3, 2):
            from_z(it, d).wait_recv()
            for copy in relays(it, d):
                copy.start()
        next_from_row(it, 0).wait_recv()
        next_to_sib(it, 0).start()
        for d in (0, 1, 3, 2):
            from_sib(it, d).wait_recv()
        ext[pl.ds(0, 32)] = xo[it]

        near_phase(0, False)
        for d in (1, 3):
            next_from_row(it, d).wait_recv()
            next_to_sib(it, d).start()
        far_phase(8, 0, 1)
        next_from_row(it, 2).wait_recv()
        next_to_sib(it, 2).start()
        for d in (0, 1, 3, 2):
            next_from_sib(it, d).wait_recv()
        ext[pl.ds(32, 32)] = xn[it]

        def fold_next(chunk, total):
            for c in range(2):
                for j in range(4):
                    place = chunk * 8 + c * 4 + j + 32
                    out = pn[tab[3, place]] + pf[tab[11, place]]
                    stn[it, c, chunk, j] = out.astype(BF16)
                    total += out * ext[place].astype(F32)
            return total

        total = lax.fori_loop(0, 4, fold_next, jnp.zeros((32, 256), F32))
        pair_next(it).start()

        def fold_own(chunk, total):
            for i in range(8):
                place = chunk * 8 + i
                out = pn[tab[3, place]] + pf[tab[11, place]]
                acc1[place] = out
                total += out * ext[place].astype(F32)
            return total

        total = lax.fori_loop(0, 4, fold_own, total)
        total = total * 2.0
        for j in range(4):
            r = r_ref[j]
            total += (diag_ref[pl.ds(j, 1), :] * r) * r
        ar1[it, me] = jnp.broadcast_to(to_row([lane_sum(total), gd[0], gd[1]]), (8, 128))
        for k in range(1, 8):
            dots_col(it, k).start()

        near_phase(4, True)

        pair_next(it).wait_recv()
        for chunk in range(4):
            for j in range(4):
                zsn[it, chunk, j] = (
                    stn[it, core, chunk, j].astype(F32) + prn[it, chunk, j].astype(F32)
                ).astype(BF16)
        for d in (1, 3, 2, 0):
            terms_next(it, d).start()
        row = jnp.zeros((8, 128), F32)
        for k in range(1, 8):
            dots_col_in(it, k).wait_recv()
        for k in range(8):
            row += ar1[it, k]
        ar2[it, g] = row
        for k in range(1, 16):
            dots_row(it, k).start()

        far_phase(12, 1, 0)

        def fold_rows(chunk, carry):
            for c in range(2):
                for j in range(4):
                    place = chunk * 8 + c * 4 + j
                    out = acc1[place] + (pn[tab[7, place]] + pf[tab[15, place]])
                    sto[it, c, chunk, j] = out.astype(BF16)
            return carry

        lax.fori_loop(0, 4, fold_rows, 0)
        pair_own(it).start()
        pair_own(it).wait_recv()
        for chunk in range(4):
            for j in range(4):
                zso[it, chunk, j] = (
                    sto[it, core, chunk, j].astype(F32) + pro[it, chunk, j].astype(F32)
                ).astype(BF16)
        for d in (1, 3, 2):
            terms_own(it, d).start()

        row = jnp.zeros((8, 128), F32)
        for k in range(1, 16):
            dots_row_in(it, k).wait_recv()
        for k in range(16):
            row += ar2[it, k]
        row = row[:1]
        delta, gamma, eta = to_col(row, 0), to_col(row, 1), to_col(row, 2)
        beta = gamma / sc[0][:, :1]
        curvature = delta + 2.0 * beta * eta + beta * beta * sc[1][:, :1]
        alpha = gamma / curvature
        sc[0] = wide(gamma)
        sc[1] = wide(curvature)

        for d in range(4):
            terms_next(it, d).wait_recv()
        for d in range(1, 4):
            terms_own(it, d).wait_recv()
        total = jnp.zeros((32, 256), F32)
        cross = jnp.zeros((32, 256), F32)
        for j in range(4):
            r = r_ref[j]
            w = diag_ref[pl.ds(j, 1), :] * r
            w += sto[it, core, z, j].astype(F32) + pro[it, z, j].astype(F32)
            for d in range(4):
                w += rn[it, d, j].astype(F32)
            for d in range(3):
                w += ro[it, d, j].astype(F32)
            p = r + beta * p_ref[j]
            q = w + beta * q_ref[j]
            p_ref[j] = p
            q_ref[j] = q
            x_ref[j] = x_ref[j] + alpha * p
            r = r - alpha * q
            r_ref[j] = r

            @pl.when(it < ITERS - 1)
            def _():
                xo[lax.min(it + 1, ITERS - 1), me * 4 + j] = r.astype(BF16)

            total += r * r
            cross += r * q

        @pl.when(it < ITERS - 1)
        def _():
            for copy in first_sends(it + 1):
                copy.start()

        gd[0] = wide(lane_sum(total))
        gd[1] = wide(lane_sum(cross))
        return carry

    lax.fori_loop(0, ITERS, iteration, 0)

    def drain(it, carry):
        for copy in first_sends(it):
            copy.wait_send()
        for d in (1, 2, 3):
            for copy in relays(it, d):
                copy.wait_send()
            terms_own(it, d).wait_send()
        for d in range(4):
            next_to_sib(it, d).wait_send()
            terms_next(it, d).wait_send()
        pair_next(it).wait_send()
        pair_own(it).wait_send()
        for k in range(1, 8):
            dots_col(it, k).wait_send()
        for k in range(1, 16):
            dots_row(it, k).wait_send()
        return carry

    lax.fori_loop(0, ITERS, drain, 0)


def body(right_side, diag_term, near_pairs, near_tiles, far_pairs, far_factors):
    offset = lax.axis_index("row") * 32
    tables = make_tables(near_pairs, far_pairs, offset)
    k_near, k_far = near_tiles.shape[0], far_factors.shape[0]
    field = jax.ShapeDtypeStruct((4, 32, 256), F32)
    vmem = pl.BlockSpec(memory_space=pltpu.VMEM)
    hbm = pl.BlockSpec(memory_space=pl.ANY)
    return pl.pallas_call(
        kernel,
        out_shape=(field, field),
        in_specs=[pl.BlockSpec(memory_space=pltpu.SMEM), vmem, vmem, hbm, hbm],
        out_specs=(vmem, vmem),
        scratch_shapes=[
            pltpu.VMEM((k_near, 256, 256), BF16),
            pltpu.VMEM((k_far, 2, 32, 256), BF16),
            pltpu.VMEM((k_near + 1, 32, 256), F32),
            pltpu.VMEM((k_far + 1, 32, 256), F32),
            pltpu.VMEM((ITERS, 32, 32, 256), BF16),
            pltpu.VMEM((ITERS, 32, 32, 256), BF16),
            pltpu.VMEM((64, 32, 256), BF16),
            pltpu.VMEM((32, 32, 256), F32),
            pltpu.VMEM((ITERS, 2, 4, 4, 32, 256), BF16),
            pltpu.VMEM((ITERS, 2, 4, 4, 32, 256), BF16),
            pltpu.VMEM((ITERS, 4, 4, 32, 256), BF16),
            pltpu.VMEM((ITERS, 4, 4, 32, 256), BF16),
            pltpu.VMEM((ITERS, 4, 4, 32, 256), BF16),
            pltpu.VMEM((ITERS, 4, 4, 32, 256), BF16),
            pltpu.VMEM((ITERS, 4, 4, 32, 256), BF16),
            pltpu.VMEM((ITERS, 3, 4, 32, 256), BF16),
            pltpu.VMEM((ITERS, 8, 8, 128), F32),
            pltpu.VMEM((ITERS, 16, 8, 128), F32),
            pltpu.VMEM((4, 32, 256), F32),
            pltpu.VMEM((4, 32, 256), F32),
            pltpu.VMEM((2, 32, 128), F32),
            pltpu.VMEM((2, 32, 128), F32),
            pltpu.SemaphoreType.DMA((ITERS, N_SEM)),
            pltpu.SemaphoreType.DMA((ITERS, N_SEM)),
            pltpu.SemaphoreType.DMA((2,)),
        ],
        compiler_params=pltpu.CompilerParams(
            collective_id=0, has_side_effects=True, vmem_limit_bytes=60 * 2**20
        ),
    )(tables, right_side, diag_term, near_tiles, far_factors)


def solution(mesh):
    placed = (
        P(("row", "col"), None, None),
        P(("row", "col"), None),
        P(None, ("row", "col")),
        P(("row", "col"), None, None),
        P(None, ("row", "col")),
        P(("row", "col"), None, None, None),
    )
    return jax.shard_map(
        body,
        mesh=mesh,
        in_specs=placed,
        out_specs=(P(("row", "col"), None, None), P(("row", "col"), None, None)),
        check_vma=False,
    )
```

time: 1060 us -> 104 us (0.10); the launches traced: 1050 us -> 104 us
  blocking collectives: 374 us -> 0 us
  waiting for transfers between devices: 272 us -> 0 us
  starting transfers between devices: 157 us -> 0 us
  other arithmetic: 108 us -> 4.3 us
  Pallas kernels: 0 us -> 94.5 us
  local copies, waits for them, and re-layouts: 68.6 us -> 4.42 us
  matrix products: 54.6 us -> 0 us
  between operations: 15.4 us -> 0.83 us
    psum x5 -> x0, blocking collectives: 328 us -> none  [the longest x3 193 us: residual_norm(): return lax.psum(jnp.sum(field * field, axis=(0, 2)), ('row', 'col'))]
    reduce_scatter x3 -> x0, waiting for transfers between devices: 223 us -> none  [body(): lax.psum_scatter(summed[:group_size] + carried, 'col', scatter_dimension=...]
    ppermute x6 -> x0, starting transfers between devices: 157 us -> none  [shifted(): lax.ppermute(value, axis, [(source, source + steps) for source in range(l...]
    pallas_call x0 -> x1, Pallas kernels: none -> 94.5 us  [body(): pl.pallas_call(kernel, out_shape=(field, field), in_specs=[pl.BlockSpec(m...]
    scatter-add x24 -> x0, other arithmetic: 73.8 us -> none  [one_turn(): return acc.at[row_ids].add(to_row * weight).at[col_ids].add(to_col * weight)]
    dot_general x24 -> x0, matrix products: 54.6 us -> none  [the longest x6 18.6 us: near_apply(): jnp.einsum('bnj,bij->bni', from_col, tile_block, preferred_element_type=j...]
    ppermute x6 -> x0, waiting for transfers between devices: 49.1 us -> none  [shifted(): lax.ppermute(value, axis, [(source, source + steps) for source in range(l...]
    all_gather x3 -> x0, blocking collectives: 45.9 us -> none  [body(): own_group = lax.all_gather(rounded, 'col', axis=0, tiled=True)]
  transfers between devices with their start and end apart: 9 -> 0, of which waited for: 9 -> 0; matrix products, arithmetic and copies ran while one was open for 1% -> 0% of each run, Pallas kernels for 0% -> 0%
where the time goes in v1:
time: 104 us
  Pallas kernels  94.5 us (91%)
  local copies, waits for them, and re-layouts  4.42 us (4%)
  other arithmetic  4.3 us (4%)
    pallas_call x1, Pallas kernels, body(): pl.pallas_call(kernel, out_shape=(field, field), in_specs=[pl.BlockSpec(m...  94.5 us
    unnamed x2, local copies, waits for them, and re-layouts  3.14 us

profile of v1, /device:TPU:1, one launch (start us, length us, event | category | flops | bytes accessed | tf_op | source)
XLA Modules:
  0.0 104.0 jit_solution(878261775239840955)
XLA Ops:
  0.6 0.8 bitcast_select_fusion.2
  1.4 0.8 bitcast_select_fusion
  2.2 0.1 convert_reduce_fusion.2
  2.4 0.8 fusion.8
  3.2 0.8 fusion.10
  4.0 0.2 convert_reduce_fusion
  4.2 0.2 convert_reduce_fusion.1
  4.4 0.2 select_reduce_fusion
  4.6 0.2 convert_reduce_fusion.6
  4.9 0.1 select_reduce_fusion.6
  5.0 0.1 select_reduce_fusion.9
  5.2 1.2 %stack.67.tab = s32[16,128]{1,0:T(8,128)} concatenate(s32[1,128]{1,0:T(1,128)S(1)} %pad_bitcast_fusion.15, s32[1,128]{1,0:T(1,128)S(1)} %pad_bitcast_fusion.14, s32[1,128]{1,0:T(1,128)S(1)} %pad_bitcast_fusion.13, s32[1,128]{1,0:T(1,128)S(1)} %pad_bitcast_fusion.12, s32[1,128]{1,0:T(1,128)S(1)} %pad_bitcast_fusion.11, s32[1,128]{1,0:T(1,128)S(1)} %pad_bitcast_fusion.10, ...), dimensions={0} | concatenate | bytes 16384 | tf_op jit(solution)/shard_map/stack | solution.py:56
  6.4 94.5 %shard_map.77 = (f32[4,32,256]{2,1,0:T(8,128)}, f32[4,32,256]{2,1,0:T(8,128)}) custom-call(s32[16,128]{1,0:T(8,128)} %stack.67.tab, f32[4,32,256]{2,1,0:T(8,128)} %b_ref.1, f32[4,256]{1,0:T(4,128)} %diag_ref.1, bf16[64,256,256]{2,1,0:T(8,128)(2,1)} %tiles_hbm.1, bf16[96,2,32,256]{3,2,1,0:T(8,128)(2,1)} %fac_hbm.1), custom_call_target="tpu_custom_call" | custom-call | tf_op jit(solution)/shard_map/pallas_call | solution.py:423
  100.9 1.6 %copy.10 = f32[4,32,256]{2,1,0:T(8,128)} copy(f32[4,32,256]{2,1,0:T(8,128)} %get-tuple-element.46) | data formatting | bytes 262144
  102.5 1.6 %copy.11 = f32[4,32,256]{2,1,0:T(8,128)} copy(f32[4,32,256]{2,1,0:T(8,128)} %get-tuple-element.47) | data formatting | bytes 262144
  (20 shorter events, 0.1 us)

commit v2 on v1

v2 whole, which is shorter than its diff:
```python
import functools

import jax
import jax.numpy as jnp
from jax import lax
from jax.experimental import pallas as pl
from jax.experimental.pallas import tpu as pltpu
from jax.sharding import PartitionSpec as P

ITERS = 3
MESH = pl.DeviceIdType.MESH
NEAR_UNROLL = 32
FAR_UNROLL = 12
F32 = jnp.float32
BF16 = jnp.bfloat16

XO_Z = 0
XO_SIB = 3
XN_ROW = 7
XN_SIB = 11
PR_NEXT = 15
PR_OWN = 16
RNZ = 17
RN = 20
RF = 46
RO = 21
AR_COL = 24
AR_ROW = 31
N_SEM = 47


def sorted_tables(key, source, dummy):
    sub = lax.broadcasted_iota(jnp.int32, (128, 128), 0)
    lane = lax.broadcasted_iota(jnp.int32, (128, 128), 1)
    eye = sub == lane
    packed = key + 128 * source + 16384 * lane[:1]
    column = jnp.sum(jnp.where(eye, packed, 0), axis=1, keepdims=True)
    key_col = column & 127
    before = (key < key_col) | ((key == key_col) & (lane < sub))
    rank = jnp.sum(before.astype(jnp.int32), axis=1, keepdims=True)
    ordered = jnp.sum(jnp.where(rank == lane, column, 0), axis=0, keepdims=True)
    upto = jnp.sum((key_col <= lane).astype(jnp.int32), axis=0, keepdims=True)
    equal = jnp.sum((key_col == lane).astype(jnp.int32), axis=0, keepdims=True)
    last = jnp.where(equal > 0, upto - 1, dummy)
    return [ordered >> 14, (ordered >> 7) & 127, ordered & 127, last]


def kernel(
    b_ref, diag_ref, near_pairs, far_pairs, tiles_hbm, fac_hbm, x_ref, r_ref,
    tiles, turned, fac, pn, pf, pn2, pf2, xo, xn, ext, acc1, stn, sto, prn, pro, zsn, zso, rnz, xs, rn, rf, ro, ar1, ar2,
    p_ref, q_ref, gd, sc, pairs, tabv, tab, ss, rs, ls,
):
    g = lax.axis_index("row")
    me = lax.axis_index("col")
    n_row = lax.axis_size("row")
    n_col = lax.axis_size("col")
    z, core = me // 2, lax.rem(me, 2)
    n_z = n_col // 2
    sib = z * 2 + (1 - core)
    nxt, prv = lax.rem(g + 1, n_row), lax.rem(g + n_row - 1, n_row)
    at_z = [lax.rem(z + d, n_z) for d in range(n_z)]
    at_col = [lax.rem(me + k, n_col) for k in range(n_col)]
    at_row = [lax.rem(g + k, n_row) for k in range(n_row)]
    k_near = tiles.shape[0]
    k_far = fac.shape[0]

    def zc(d):
        return at_z[d % n_z] * 2 + core

    def zs(d):
        return at_z[d % n_z] * 2 + (1 - core)

    def rdma(it, idx, src, dst, row, col):
        return pltpu.make_async_remote_copy(
            src_ref=src, dst_ref=dst, send_sem=ss.at[it, idx], recv_sem=rs.at[it, idx],
            device_id=(row, col), device_id_type=MESH,
        )

    def shard(ref, it, col):
        return ref.at[it, pl.ds(col * 4, 4)]

    load_tiles = pltpu.make_async_copy(tiles_hbm, tiles, ls.at[0])
    load_fac = pltpu.make_async_copy(fac_hbm, fac, ls.at[1])
    load_tiles.start()
    load_fac.start()

    barrier = pltpu.get_barrier_semaphore()
    peers = [(g, at_col[k]) for k in range(1, n_col)]
    peers += [(at_row[k], me) for k in range(1, n_row)]
    for peer in peers:
        pl.semaphore_signal(barrier, inc=1, device_id=peer, device_id_type=MESH)

    sub = lax.broadcasted_iota(jnp.int32, (32, 128), 0)
    lane = lax.broadcasted_iota(jnp.int32, (32, 128), 1)

    def lane_sum(field):
        return jnp.sum(field[:, :128] + field[:, 128:], axis=1, keepdims=True)

    def to_row(cols):
        total = jnp.zeros((32, 128), F32)
        for j, col in enumerate(cols):
            total += jnp.where(lane == sub + 32 * j, col, 0.0)
        return jnp.sum(total, axis=0, keepdims=True)

    def to_col(row, j):
        return jnp.sum(jnp.where(lane == sub + 32 * j, row, 0.0), axis=1, keepdims=True)

    def wide(col):
        return jnp.broadcast_to(col, (32, 128))

    total = jnp.zeros((32, 256), F32)
    for j in range(4):
        r = b_ref[j]
        r_ref[j] = r
        x_ref[j] = jnp.zeros((32, 256), F32)
        p_ref[j] = jnp.zeros((32, 256), F32)
        q_ref[j] = jnp.zeros((32, 256), F32)
        xo[0, me * 4 + j] = r.astype(BF16)
        total += r * r
    gd[0] = wide(lane_sum(total))
    gd[1] = jnp.zeros((32, 128), F32)
    sc[0] = jnp.ones((32, 128), F32)
    sc[1] = jnp.zeros((32, 128), F32)
    for ref in (pn, pn2):
        ref[k_near] = jnp.zeros((32, 256), F32)
    for ref in (pf, pf2):
        ref[k_far] = jnp.zeros((32, 256), F32)

    pairs[...] = jnp.zeros((8, 128), jnp.int32)
    pairs[pl.ds(0, 3), pl.ds(0, k_near)] = near_pairs[...]
    pairs[pl.ds(3, 3), pl.ds(0, k_far)] = far_pairs[...]
    tables = []
    for first, count in ((0, k_near), (3, k_far)):
        row_id = jnp.clip(pairs[pl.ds(first, 1), :] - g * 32, 0, 31)
        col_id = jnp.clip(pairs[pl.ds(first + 1, 1), :] - g * 32, 0, 63)
        live = pairs[pl.ds(first + 2, 1), :] != 0
        tables += sorted_tables(jnp.where(live, col_id, 64), row_id, count)
        tables += sorted_tables(jnp.where(live, row_id, 64), col_id, count)
    for i, line in enumerate(tables):
        tabv[pl.ds(i, 1), :] = line
    copy_tab = pltpu.make_async_copy(tabv, tab, ls.at[2])
    copy_tab.start()

    pl.semaphore_wait(barrier, len(peers))

    def first_sends(it):
        mine = shard(xo, it, me)
        return [
            rdma(it, XO_Z + d - 1, mine, mine, g, zc(d)) for d in (1, 3, 2)
        ] + [
            rdma(it, XO_SIB, mine, mine, g, sib),
            rdma(it, XN_ROW, mine, shard(xn, it, me), prv, me),
        ]

    def from_z(it, d):
        here = shard(xo, it, zc(-d))
        return rdma(it, XO_Z + d - 1, here, here, g, zc(d))

    def relays(it, d):
        here = shard(xo, it, zc(-d))
        copies = [rdma(it, XO_SIB + d, here, here, g, sib)]
        if d == 2:
            copies.append(rdma(it, XN_ROW + d, here, shard(xn, it, zc(-d)), prv, me))
        return copies

    def next_to_z(it, d):
        here = shard(xn, it, me)
        return rdma(it, XN_ROW + d, here, here, g, zc(d))

    def from_sib(it, d):
        here = shard(xo, it, zs(-d))
        return rdma(it, XO_SIB + d, here, here, g, sib)

    def next_from_row(it, d):
        here = shard(xn, it, zc(-d))
        return rdma(it, XN_ROW + d, here, here, prv, me)

    def next_to_sib(it, d):
        here = shard(xn, it, zc(-d))
        return rdma(it, XN_SIB + d, here, here, g, sib)

    def next_from_sib(it, d):
        here = shard(xn, it, zs(-d))
        return rdma(it, XN_SIB + d, here, here, g, sib)

    def pair_next(it):
        return rdma(it, PR_NEXT, stn.at[it, 1 - core], prn.at[it], g, sib)

    def pair_own(it):
        return rdma(it, PR_OWN, sto.at[it, 1 - core], pro.at[it], g, sib)

    def terms_next(it, d):
        return rdma(it, RNZ + d - 1, zsn.at[it, d - 1], rnz.at[it, d - 1], g, zc(d))

    def terms_far(it):
        return rdma(it, RF, zsn.at[it, 1], rf.at[it], nxt, me)

    def terms_over(it):
        return rdma(it, RN, xs.at[it], rn.at[it], nxt, me)

    def terms_own(it, d):
        return rdma(it, RO + d - 1, zso.at[it, d - 1], ro.at[it, d - 1], g, zc(d))

    def dots_col(it, k):
        return rdma(it, AR_COL + k - 1, ar1.at[it, me], ar1.at[it, me], g, at_col[k])

    def dots_col_in(it, k):
        here = ar1.at[it, at_col[n_col - k]]
        return rdma(it, AR_COL + k - 1, here, here, g, at_col[k])

    def dots_row(it, k):
        return rdma(it, AR_ROW + k - 1, ar2.at[it, g], ar2.at[it, g], at_row[k], me)

    def dots_row_in(it, k):
        here = ar2.at[it, at_row[n_row - k]]
        return rdma(it, AR_ROW + k - 1, here, here, at_row[k], me)

    def near_phase(base, blocks, sums, first, last, acc):
        def step(block, acc):
            for u in range(NEAR_UNROLL):
                k = block * NEAR_UNROLL + u
                field = ext[tab[base + 1, k]]
                tile = blocks[tab[base, k]]
                keep = (tab[base + 2, k] == tab[base + 2, lax.max(k - 1, 0)]).astype(F32)
                term = lax.dot_general(field, tile, (((1,), (0,)), ((), ())), preferred_element_type=F32)
                acc = acc * keep + term
                sums[k] = acc
            return acc

        return lax.fori_loop(first // NEAR_UNROLL, last // NEAR_UNROLL, step, acc)

    def far_phase(base, first, second, sums):
        lanes = lax.broadcasted_iota(jnp.int32, (256, 256), 1) // 32
        rows = lax.broadcasted_iota(jnp.int32, (256, 256), 0) // 32
        mask = lanes == rows

        def step(block, acc):
            for u in range(FAR_UNROLL):
                start = (block * FAR_UNROLL + u) * 8
                fields, lefts, rights = [], [], []
                for q in range(8):
                    slot = tab[base, start + q]
                    fields.append(ext[tab[base + 1, start + q]])
                    lefts.append(fac[slot, first])
                    rights.append(fac[slot, second])
                field = jnp.concatenate(fields, axis=0)
                left = jnp.concatenate(lefts, axis=0)
                right = jnp.concatenate(rights, axis=0)
                inner = lax.dot_general(field, left, (((1,), (1,)), ((), ())), preferred_element_type=F32)
                inner = jnp.where(mask, inner, 0.0).astype(BF16)
                term = lax.dot_general(inner, right, (((1,), (0,)), ((), ())), preferred_element_type=F32)
                for q in range(8):
                    k = start + q
                    keep = (tab[base + 2, k] == tab[base + 2, lax.max(k - 1, 0)]).astype(F32)
                    acc = acc * keep + term[q * 32 : q * 32 + 32]
                    sums[k] = acc
            return acc

        lax.fori_loop(0, k_far // (8 * FAR_UNROLL), step, jnp.zeros((32, 256), F32))

    for copy in first_sends(0):
        copy.start()
    copy_tab.wait()
    load_tiles.wait()

    def turn(block, carry):
        for u in range(4):
            turned[block * 4 + u] = tiles[block * 4 + u].T
        return carry

    lax.fori_loop(0, k_near // 4, turn, 0)
    load_fac.wait()

    def iteration(it, carry):
        for d in (1, 3):
            from_z(it, d).wait_recv()
            for copy in relays(it, d):
                copy.start()
        next_from_row(it, 0).wait_recv()
        for d in (1, 3):
            next_to_z(it, d).start()
        from_z(it, 2).wait_recv()
        for copy in relays(it, 2):
            copy.start()
        next_to_sib(it, 0).start()
        for d in (0, 1, 3, 2):
            from_sib(it, d).wait_recv()
        ext[pl.ds(0, 32)] = xo[it]

        zero = jnp.zeros((32, 256), F32)
        far_phase(8, 0, 1, pf)
        acc = near_phase(0, tiles, pn, 0, k_near // 2, zero)
        for d in (1, 3, 2):
            next_from_row(it, d).wait_recv()
            next_to_sib(it, d).start()
        near_phase(0, tiles, pn, k_near // 2, k_near, acc)

        def fold_next(chunk, carry):
            for c in range(2):
                for j in range(4):
                    place = chunk * 8 + c * 4 + j + 32
                    out = pn[tab[3, place]] + pf[tab[11, place]]
                    acc1[place] = out
                    stn[it, c, chunk, j] = out.astype(BF16)
            return carry

        lax.fori_loop(0, 4, fold_next, 0)
        pair_next(it).start()

        for d in (0, 1, 3, 2):
            next_from_sib(it, d).wait_recv()
        ext[pl.ds(32, 32)] = xn[it]

        acc = near_phase(4, turned, pn2, 0, k_near // 2, zero)

        pair_next(it).wait_recv()
        for d in (2, 1, 3):
            chunk = at_z[d]
            for j in range(4):
                zsn[it, d - 1, j] = (
                    stn[it, core, chunk, j].astype(F32) + prn[it, chunk, j].astype(F32)
                ).astype(BF16)
            (terms_far(it) if d == 2 else terms_next(it, d)).start()

        def fold_own(chunk, total):
            for i in range(8):
                place = chunk * 8 + i
                out = pn[tab[3, place]] + pf[tab[11, place]]
                acc1[place] = out
                total += out * ext[place].astype(F32)
            return total

        total = lax.fori_loop(0, 4, fold_own, zero)
        def dot_next(chunk, total):
            for i in range(8):
                place = chunk * 8 + i + 32
                total += acc1[place] * ext[place].astype(F32)
            return total

        total = lax.fori_loop(0, 4, dot_next, total) * 2.0
        for j in range(4):
            r = r_ref[j]
            total += (diag_ref[pl.ds(j, 1), :] * r) * r
        ar1[it, me] = to_row([lane_sum(total), gd[0], gd[1]])
        for k in range(1, 8):
            dots_col(it, k).start()

        far_phase(12, 1, 0, pf2)
        near_phase(4, turned, pn2, k_near // 2, k_near, acc)

        def fold_rows(chunk, c):
            for j in range(4):
                place = chunk * 8 + c * 4 + j
                out = acc1[place] + (pn2[tab[7, place]] + pf2[tab[15, place]])
                sto[it, c, chunk, j] = out.astype(BF16)
            return c

        lax.fori_loop(0, 4, fold_rows, 1 - core)
        pair_own(it).start()
        lax.fori_loop(0, 4, fold_rows, core)
        row = jnp.zeros((1, 128), F32)
        for k in range(1, 8):
            dots_col_in(it, k).wait_recv()
        for k in range(8):
            row += ar1[it, k]
        ar2[it, g] = row
        for k in range(1, 16):
            dots_row(it, k).start()
        pair_own(it).wait_recv()
        for d in (1, 3, 2):
            chunk = at_z[d]
            if d == 2:
                terms_far(it).wait_recv()
            for j in range(4):
                out = sto[it, core, chunk, j].astype(F32) + pro[it, chunk, j].astype(F32)
                if d == 2:
                    out += rf[it, j].astype(F32)
                zso[it, d - 1, j] = out.astype(BF16)
            terms_own(it, d).start()

        for d in (1, 3):
            terms_next(it, d).wait_recv()
        for j in range(4):
            out = stn[it, core, z, j].astype(F32) + prn[it, z, j].astype(F32)
            for d in (0, 2):
                out += rnz[it, d, j].astype(F32)
            xs[it, j] = out.astype(BF16)
        terms_over(it).start()

        row = jnp.zeros((1, 128), F32)
        for k in range(1, 16):
            dots_row_in(it, k).wait_recv()
        for k in range(16):
            row += ar2[it, k]
        delta, gamma, eta = to_col(row, 0), to_col(row, 1), to_col(row, 2)
        beta = gamma / sc[0][:, :1]
        curvature = delta + 2.0 * beta * eta + beta * beta * sc[1][:, :1]
        alpha = gamma / curvature
        sc[0] = wide(gamma)
        sc[1] = wide(curvature)

        for j in range(4):
            r = r_ref[j]
            p = r + beta * p_ref[j]
            p_ref[j] = p
            x_ref[j] = x_ref[j] + alpha * p
            q = diag_ref[pl.ds(j, 1), :] * r + beta * q_ref[j]
            q_ref[j] = q + (sto[it, core, z, j].astype(F32) + pro[it, z, j].astype(F32))
        for d in (1, 3, 2):
            terms_own(it, d).wait_recv()
        terms_over(it).wait_recv()
        total = jnp.zeros((32, 256), F32)
        cross = jnp.zeros((32, 256), F32)
        for j in range(4):
            q = q_ref[j] + rn[it, j].astype(F32)
            for d in range(3):
                q += ro[it, d, j].astype(F32)
            q_ref[j] = q
            r = r_ref[j] - alpha * q
            r_ref[j] = r

            @pl.when(it < ITERS - 1)
            def _():
                xo[lax.min(it + 1, ITERS - 1), me * 4 + j] = r.astype(BF16)

            total += r * r
            cross += r * q

        @pl.when(it < ITERS - 1)
        def _():
            for copy in first_sends(it + 1):
                copy.start()

        gd[0] = wide(lane_sum(total))
        gd[1] = wide(lane_sum(cross))
        return carry

    lax.fori_loop(0, ITERS, iteration, 0)

    def drain(it, carry):
        for copy in first_sends(it):
            copy.wait_send()
        for d in (1, 2, 3):
            for copy in relays(it, d):
                copy.wait_send()
            terms_own(it, d).wait_send()
        for d in (1, 3):
            next_to_z(it, d).wait_send()
            terms_next(it, d).wait_send()
        terms_far(it).wait_send()
        terms_over(it).wait_send()
        for d in range(4):
            next_to_sib(it, d).wait_send()
        pair_next(it).wait_send()
        pair_own(it).wait_send()
        for k in range(1, 8):
            dots_col(it, k).wait_send()
        for k in range(1, 16):
            dots_row(it, k).wait_send()
        return carry

    lax.fori_loop(0, ITERS, drain, 0)


def body(right_side, diag_term, near_pairs, near_tiles, far_pairs, far_factors):
    k_near, k_far = near_tiles.shape[0], far_factors.shape[0]
    field = jax.ShapeDtypeStruct((4, 32, 256), F32)
    vmem = pl.BlockSpec(memory_space=pltpu.VMEM)
    hbm = pl.BlockSpec(memory_space=pl.ANY)
    xa, ra = pl.pallas_call(
        kernel,
        out_shape=(field, field),
        in_specs=[vmem, vmem, vmem, vmem, hbm, hbm],
        out_specs=(vmem, vmem),
        scratch_shapes=[
            pltpu.VMEM((k_near, 256, 256), BF16),
            pltpu.VMEM((k_near, 256, 256), BF16),
            pltpu.VMEM((k_far, 2, 32, 256), BF16),
            pltpu.VMEM((k_near + 1, 32, 256), F32),
            pltpu.VMEM((k_far + 1, 32, 256), F32),
            pltpu.VMEM((k_near + 1, 32, 256), F32),
            pltpu.VMEM((k_far + 1, 32, 256), F32),
            pltpu.VMEM((ITERS, 32, 32, 256), BF16),
            pltpu.VMEM((ITERS, 32, 32, 256), BF16),
            pltpu.VMEM((64, 32, 256), BF16),
            pltpu.VMEM((64, 32, 256), F32),
            pltpu.VMEM((ITERS, 2, 4, 4, 32, 256), BF16),
            pltpu.VMEM((ITERS, 2, 4, 4, 32, 256), BF16),
            pltpu.VMEM((ITERS, 4, 4, 32, 256), BF16),
            pltpu.VMEM((ITERS, 4, 4, 32, 256), BF16),
            pltpu.VMEM((ITERS, 3, 4, 32, 256), BF16),
            pltpu.VMEM((ITERS, 3, 4, 32, 256), BF16),
            pltpu.VMEM((ITERS, 3, 4, 32, 256), BF16),
            pltpu.VMEM((ITERS, 4, 32, 256), BF16),
            pltpu.VMEM((ITERS, 4, 32, 256), BF16),
            pltpu.VMEM((ITERS, 4, 32, 256), BF16),
            pltpu.VMEM((ITERS, 3, 4, 32, 256), BF16),
            pltpu.VMEM((ITERS, 8, 1, 128), F32),
            pltpu.VMEM((ITERS, 16, 1, 128), F32),
            pltpu.VMEM((4, 32, 256), F32),
            pltpu.VMEM((4, 32, 256), F32),
            pltpu.VMEM((2, 32, 128), F32),
            pltpu.VMEM((2, 32, 128), F32),
            pltpu.VMEM((8, 128), jnp.int32),
            pltpu.VMEM((16, 128), jnp.int32),
            pltpu.SMEM((16, 128), jnp.int32),
            pltpu.SemaphoreType.DMA((ITERS, N_SEM)),
            pltpu.SemaphoreType.DMA((ITERS, N_SEM)),
            pltpu.SemaphoreType.DMA((3,)),
        ],
        compiler_params=pltpu.CompilerParams(
            collective_id=0, has_side_effects=True, vmem_limit_bytes=60 * 2**20
        ),
    )(right_side, diag_term, near_pairs, far_pairs, near_tiles, far_factors)

    def tail(a, b, c, d):
        c[...] = a[...]
        d[...] = b[...]

    return pl.pallas_call(tail, out_shape=(field, field), in_specs=[vmem, vmem], out_specs=(vmem, vmem))(xa, ra)


def solution(mesh):
    placed = (
        P(("row", "col"), None, None),
        P(("row", "col"), None),
        P(None, ("row", "col")),
        P(("row", "col"), None, None),
        P(None, ("row", "col")),
        P(("row", "col"), None, None, None),
    )
    return jax.shard_map(
        body,
        mesh=mesh,
        in_specs=placed,
        out_specs=(P(("row", "col"), None, None), P(("row", "col"), None, None)),
        check_vma=False,
    )
```

time: 104 us -> 80.5 us (0.77)
  Pallas kernels: 94.5 us -> 79.7 us
  local copies, waits for them, and re-layouts: 4.42 us -> 0 us
  other arithmetic: 4.3 us -> 0 us
    pallas_call x1 -> x2, Pallas kernels: 94.5 us -> 79.7 us  [the longest x1 78.1 us: body(): pl.pallas_call(kernel, out_shape=(field, field), in_specs=[vmem, vmem, vm...]
    unnamed x2 -> x0, local copies, waits for them, and re-layouts: 3.14 us -> none
    select_n x6 -> x0, other arithmetic: 1.62 us -> none  [the longest x2 1.6 us: make_tables(): rows += sorted_tables(jnp.where(live, row, 64), col, count)]
    min x2 -> x0, other arithmetic: 1.6 us -> none  [make_tables(): col = jnp.clip(pairs[1] - offset, 0, 63)]
    another operation x17 -> x0, local copies, waits for them, and re-layouts: 1.29 us -> none  [make_tables(): return jnp.stack(rows)]
    reduce_sum x7 -> x0, other arithmetic: 1.08 us -> none  [the longest x3 0.38 us: sorted_tables(): skey = jnp.sum(hit * key[:, None], axis=0)]
where the time goes in v2:
time: 80.5 us; the launch traced here: 80.4 us
  Pallas kernels  79.7 us (99%)
    pallas_call x1, Pallas kernels, body(): pl.pallas_call(kernel, out_shape=(field, field), in_specs=[vmem, vmem, vm...  78.1 us
    pallas_call x1, Pallas kernels, body(): pl.pallas_call(tail, out_shape=(field, field), in_specs=[vmem, vmem], out...  1.68 us

profile of v2, /device:TPU:1, one launch (start us, length us, event | category | flops | bytes accessed | tf_op | source)
XLA Modules:
  0.0 80.4 jit_solution(1555660283604141686)
XLA Ops:
  0.6 78.1 %shard_map.77 = (f32[4,32,256]{2,1,0:T(8,128)}, f32[4,32,256]{2,1,0:T(8,128)}) custom-call(f32[4,32,256]{2,1,0:T(8,128)} %b_ref.1, f32[4,256]{1,0:T(4,128)} %diag_ref.1, s32[3,64]{1,0:T(4,128)} %near_pairs.1, s32[3,96]{1,0:T(4,128)} %far_pairs.1, bf16[64,256,256]{2,1,0:T(8,128)(2,1)} %tiles_hbm.1, bf16[96,2,32,256]{3,2,1,0:T(8,128)(2,1)} %fac_hbm.1), custom_call_target="tpu_custom_call" | custom-call | tf_op jit(solution)/shard_map/pallas_call | solution.py:470
  78.7 1.7 %shard_map.78 = (f32[4,32,256]{2,1,0:T(8,128)}, f32[4,32,256]{2,1,0:T(8,128)}) custom-call(f32[4,32,256]{2,1,0:T(8,128)} %get-tuple-element.4.a, f32[4,32,256]{2,1,0:T(8,128)} %get-tuple-element.5.b), custom_call_target="tpu_custom_call" | custom-call | tf_op jit(solution)/shard_map/pallas_call | solution.py:520

commit v3 on v2

--- a/solution.py
+++ b/solution.py
@@ -48,7 +48,7 @@
 def kernel(
     b_ref, diag_ref, near_pairs, far_pairs, tiles_hbm, fac_hbm, x_ref, r_ref,
     tiles, turned, fac, pn, pf, pn2, pf2, xo, xn, ext, acc1, stn, sto, prn, pro, zsn, zso, rnz, xs, rn, rf, ro, ar1, ar2,
-    p_ref, q_ref, gd, sc, pairs, tabv, tab, ss, rs, ls,
+    p_ref, q_ref, gd, sc, dots, pairs, tabv, tab, ss, rs, ls,
 ):
     g = lax.axis_index("row")
     me = lax.axis_index("col")
@@ -146,7 +146,7 @@
     def first_sends(it):
         mine = shard(xo, it, me)
         return [
-            rdma(it, XO_Z + d - 1, mine, mine, g, zc(d)) for d in (1, 3, 2)
+            rdma(it, XO_Z + d - 1, mine, mine, g, zc(d)) for d in (2, 1, 3)
         ] + [
             rdma(it, XO_SIB, mine, mine, g, sib),
             rdma(it, XN_ROW, mine, shard(xn, it, me), prv, me),
@@ -215,10 +215,14 @@
         here = ar2.at[it, at_row[n_row - k]]
         return rdma(it, AR_ROW + k - 1, here, here, at_row[k], me)
 
-    def near_phase(base, blocks, sums, first, last, acc):
+    def near_phase(base, blocks, sums, first, last, acc, beside=None):
+        unroll = min(NEAR_UNROLL, last - first)
+
         def step(block, acc):
-            for u in range(NEAR_UNROLL):
-                k = block * NEAR_UNROLL + u
+            for u in range(unroll):
+                if beside is not None:
+                    beside(u)
+                k = first + block * unroll + u
                 field = ext[tab[base + 1, k]]
                 tile = blocks[tab[base, k]]
                 keep = (tab[base + 2, k] == tab[base + 2, lax.max(k - 1, 0)]).astype(F32)
@@ -227,7 +231,7 @@
                 sums[k] = acc
             return acc
 
-        return lax.fori_loop(first // NEAR_UNROLL, last // NEAR_UNROLL, step, acc)
+        return lax.fori_loop(0, (last - first) // unroll, step, acc)
 
     def far_phase(base, first, second, sums):
         lanes = lax.broadcasted_iota(jnp.int32, (256, 256), 1) // 32
@@ -295,23 +299,29 @@
             next_to_sib(it, d).start()
         near_phase(0, tiles, pn, k_near // 2, k_near, acc)
 
-        def fold_next(chunk, carry):
-            for c in range(2):
-                for j in range(4):
-                    place = chunk * 8 + c * 4 + j + 32
-                    out = pn[tab[3, place]] + pf[tab[11, place]]
-                    acc1[place] = out
-                    stn[it, c, chunk, j] = out.astype(BF16)
-            return carry
-
-        lax.fori_loop(0, 4, fold_next, 0)
+        def fold_next(chunk, j, c):
+            place = chunk * 8 + c * 4 + j + 32
+            out = pn[tab[3, place]] + pf[tab[11, place]]
+            acc1[place] = out
+            stn[it, c, chunk, j] = out.astype(BF16)
+
+        for chunk in range(4):
+            for j in range(4):
+                fold_next(chunk, j, 1 - core)
         pair_next(it).start()
 
         for d in (0, 1, 3, 2):
             next_from_sib(it, d).wait_recv()
         ext[pl.ds(32, 32)] = xn[it]
 
-        acc = near_phase(4, turned, pn2, 0, k_near // 2, zero)
+        dots[...] = zero
+
+        def fold_own(i):
+            out = pn[tab[3, i]] + pf[tab[11, i]]
+            acc1[i] = out
+            dots[...] += out * ext[i].astype(F32) + acc1[i + 32] * ext[i + 32].astype(F32)
+
+        acc = near_phase(4, turned, pn2, 0, 16, zero, lambda i: fold_next(i // 4, i % 4, core))
 
         pair_next(it).wait_recv()
         for d in (2, 1, 3):
@@ -322,22 +332,8 @@
                 ).astype(BF16)
             (terms_far(it) if d == 2 else terms_next(it, d)).start()
 
-        def fold_own(chunk, total):
-            for i in range(8):
-                place = chunk * 8 + i
-                out = pn[tab[3, place]] + pf[tab[11, place]]
-                acc1[place] = out
-                total += out * ext[place].astype(F32)
-            return total
-
-        total = lax.fori_loop(0, 4, fold_own, zero)
-        def dot_next(chunk, total):
-            for i in range(8):
-                place = chunk * 8 + i + 32
-                total += acc1[place] * ext[place].astype(F32)
-            return total
-
-        total = lax.fori_loop(0, 4, dot_next, total) * 2.0
+        acc = near_phase(4, turned, pn2, 16, 48, acc, fold_own)
+        total = dots[...] * 2.0
         for j in range(4):
             r = r_ref[j]
             total += (diag_ref[pl.ds(j, 1), :] * r) * r
@@ -346,7 +342,7 @@
             dots_col(it, k).start()
 
         far_phase(12, 1, 0, pf2)
-        near_phase(4, turned, pn2, k_near // 2, k_near, acc)
+        near_phase(4, turned, pn2, 48, k_near, acc)
 
         def fold_rows(chunk, c):
             for j in range(4):
@@ -501,6 +497,7 @@
             pltpu.VMEM((4, 32, 256), F32),
             pltpu.VMEM((2, 32, 128), F32),
             pltpu.VMEM((2, 32, 128), F32),
+            pltpu.VMEM((32, 256), F32),
             pltpu.VMEM((8, 128), jnp.int32),
             pltpu.VMEM((16, 128), jnp.int32),
             pltpu.SMEM((16, 128), jnp.int32),

time: 80.5 us -> 77.7 us (0.965)
  Pallas kernels: 79.7 us -> 77 us
    pallas_call x1, Pallas kernels: 78.1 us -> 75.3 us  [body(): pl.pallas_call(kernel, out_shape=(field, field), in_specs=[vmem, vmem, vm...]
where the time goes in v3:
time: 77.7 us; the launch traced here: 77.6 us
  Pallas kernels  77 us (99%)
    pallas_call x1, Pallas kernels, body(): pl.pallas_call(kernel, out_shape=(field, field), in_specs=[vmem, vmem, vm...  75.3 us
    pallas_call x1, Pallas kernels, body(): pl.pallas_call(tail, out_shape=(field, field), in_specs=[vmem, vmem], out...  1.68 us

profile of v3, /device:TPU:1, one launch (start us, length us, event | category | flops | bytes accessed | tf_op | source)
XLA Modules:
  0.0 77.6 jit_solution(6527107286047354021)
XLA Ops:
  0.6 75.3 %shard_map.77 = (f32[4,32,256]{2,1,0:T(8,128)}, f32[4,32,256]{2,1,0:T(8,128)}) custom-call(f32[4,32,256]{2,1,0:T(8,128)} %b_ref.1, f32[4,256]{1,0:T(4,128)} %diag_ref.1, s32[3,64]{1,0:T(4,128)} %near_pairs.1, s32[3,96]{1,0:T(4,128)} %far_pairs.1, bf16[64,256,256]{2,1,0:T(8,128)(2,1)} %tiles_hbm.1, bf16[96,2,32,256]{3,2,1,0:T(8,128)(2,1)} %fac_hbm.1), custom_call_target="tpu_custom_call" | custom-call | tf_op jit(solution)/shard_map/pallas_call | solution.py:466
  75.9 1.7 %shard_map.78 = (f32[4,32,256]{2,1,0:T(8,128)}, f32[4,32,256]{2,1,0:T(8,128)}) custom-call(f32[4,32,256]{2,1,0:T(8,128)} %get-tuple-element.4.a, f32[4,32,256]{2,1,0:T(8,128)} %get-tuple-element.5.b), custom_call_target="tpu_custom_call" | custom-call | tf_op jit(solution)/shard_map/pallas_call | solution.py:517

commit v4 on v3

--- a/solution.py
+++ b/solution.py
@@ -87,6 +87,7 @@
     barrier = pltpu.get_barrier_semaphore()
     peers = [(g, at_col[k]) for k in range(1, n_col)]
     peers += [(at_row[k], me) for k in range(1, n_row)]
+    peers += [(nxt, sib), (prv, sib)]
     for peer in peers:
         pl.semaphore_signal(barrier, inc=1, device_id=peer, device_id_type=MESH)
 
@@ -160,7 +161,9 @@
         here = shard(xo, it, zc(-d))
         copies = [rdma(it, XO_SIB + d, here, here, g, sib)]
         if d == 2:
-            copies.append(rdma(it, XN_ROW + d, here, shard(xn, it, zc(-d)), prv, me))
+            there = shard(xn, it, zc(-d))
+            copies.append(rdma(it, XN_ROW + d, here, there, prv, me))
+            copies.append(rdma(it, XN_SIB + d, here, there, prv, sib))
         return copies
 
     def next_to_z(it, d):
@@ -294,10 +297,10 @@
         zero = jnp.zeros((32, 256), F32)
         far_phase(8, 0, 1, pf)
         acc = near_phase(0, tiles, pn, 0, k_near // 2, zero)
-        for d in (1, 3, 2):
+        near_phase(0, tiles, pn, k_near // 2, k_near, acc)
+        for d in (1, 3):
             next_from_row(it, d).wait_recv()
             next_to_sib(it, d).start()
-        near_phase(0, tiles, pn, k_near // 2, k_near, acc)
 
         def fold_next(chunk, j, c):
             place = chunk * 8 + c * 4 + j + 32
@@ -310,6 +313,7 @@
                 fold_next(chunk, j, 1 - core)
         pair_next(it).start()
 
+        next_from_row(it, 2).wait_recv()
         for d in (0, 1, 3, 2):
             next_from_sib(it, d).wait_recv()
         ext[pl.ds(32, 32)] = xn[it]
@@ -445,7 +449,7 @@
             terms_next(it, d).wait_send()
         terms_far(it).wait_send()
         terms_over(it).wait_send()
-        for d in range(4):
+        for d in (0, 1, 3):
             next_to_sib(it, d).wait_send()
         pair_next(it).wait_send()
         pair_own(it).wait_send()

time: 77.7 us -> 76.8 us (0.988)
  Pallas kernels: 77 us -> 76 us
    pallas_call x1, Pallas kernels: 75.3 us -> 74.3 us  [body(): pl.pallas_call(kernel, out_shape=(field, field), in_specs=[vmem, vmem, vm...]
where the time goes in v4:
time: 76.8 us; the launch traced here: 76.6 us
  Pallas kernels  76 us (99%)
    pallas_call x1, Pallas kernels, body(): pl.pallas_call(kernel, out_shape=(field, field), in_specs=[vmem, vmem, vm...  74.3 us
    pallas_call x1, Pallas kernels, body(): pl.pallas_call(tail, out_shape=(field, field), in_specs=[vmem, vmem], out...  1.68 us

profile of v4, /device:TPU:1, one launch (start us, length us, event | category | flops | bytes accessed | tf_op | source)
XLA Modules:
  0.0 76.6 jit_solution(7225236299378120999)
XLA Ops:
  0.6 74.3 %shard_map.77 = (f32[4,32,256]{2,1,0:T(8,128)}, f32[4,32,256]{2,1,0:T(8,128)}) custom-call(f32[4,32,256]{2,1,0:T(8,128)} %b_ref.1, f32[4,256]{1,0:T(4,128)} %diag_ref.1, s32[3,64]{1,0:T(4,128)} %near_pairs.1, s32[3,96]{1,0:T(4,128)} %far_pairs.1, bf16[64,256,256]{2,1,0:T(8,128)(2,1)} %tiles_hbm.1, bf16[96,2,32,256]{3,2,1,0:T(8,128)(2,1)} %fac_hbm.1), custom_call_target="tpu_custom_call" | custom-call | tf_op jit(solution)/shard_map/pallas_call | solution.py:470
  75.0 1.7 %shard_map.78 = (f32[4,32,256]{2,1,0:T(8,128)}, f32[4,32,256]{2,1,0:T(8,128)}) custom-call(f32[4,32,256]{2,1,0:T(8,128)} %get-tuple-element.4.a, f32[4,32,256]{2,1,0:T(8,128)} %get-tuple-element.5.b), custom_call_target="tpu_custom_call" | custom-call | tf_op jit(solution)/shard_map/pallas_call | solution.py:521

commit v5 on v4

--- a/solution.py
+++ b/solution.py
@@ -151,6 +151,7 @@
         ] + [
             rdma(it, XO_SIB, mine, mine, g, sib),
             rdma(it, XN_ROW, mine, shard(xn, it, me), prv, me),
+            rdma(it, XN_SIB, mine, shard(xn, it, me), prv, sib),
         ]
 
     def from_z(it, d):
@@ -289,7 +290,6 @@
         from_z(it, 2).wait_recv()
         for copy in relays(it, 2):
             copy.start()
-        next_to_sib(it, 0).start()
         for d in (0, 1, 3, 2):
             from_sib(it, d).wait_recv()
         ext[pl.ds(0, 32)] = xo[it]
@@ -345,8 +345,8 @@
         for k in range(1, 8):
             dots_col(it, k).start()
 
+        near_phase(4, turned, pn2, 48, k_near, acc)
         far_phase(12, 1, 0, pf2)
-        near_phase(4, turned, pn2, 48, k_near, acc)
 
         def fold_rows(chunk, c):
             for j in range(4):
@@ -449,7 +449,7 @@
             terms_next(it, d).wait_send()
         terms_far(it).wait_send()
         terms_over(it).wait_send()
-        for d in (0, 1, 3):
+        for d in (1, 3):
             next_to_sib(it, d).wait_send()
         pair_next(it).wait_send()
         pair_own(it).wait_send()

time: 76.8 us -> 76.8 us (level)
  no operation moved by 1% of the time
where the time goes in v5:
time: 76.8 us; the launch traced here: 76.7 us
  Pallas kernels  76 us (99%)
    pallas_call x1, Pallas kernels, body(): pl.pallas_call(kernel, out_shape=(field, field), in_specs=[vmem, vmem, vm...  74.3 us
    pallas_call x1, Pallas kernels, body(): pl.pallas_call(tail, out_shape=(field, field), in_specs=[vmem, vmem], out...  1.68 us

profile of v5, /device:TPU:1, one launch (start us, length us, event | category | flops | bytes accessed | tf_op | source)
XLA Modules:
  0.0 76.7 jit_solution(1239928020961869747)
XLA Ops:
  0.6 74.3 %shard_map.77 = (f32[4,32,256]{2,1,0:T(8,128)}, f32[4,32,256]{2,1,0:T(8,128)}) custom-call(f32[4,32,256]{2,1,0:T(8,128)} %b_ref.1, f32[4,256]{1,0:T(4,128)} %diag_ref.1, s32[3,64]{1,0:T(4,128)} %near_pairs.1, s32[3,96]{1,0:T(4,128)} %far_pairs.1, bf16[64,256,256]{2,1,0:T(8,128)(2,1)} %tiles_hbm.1, bf16[96,2,32,256]{3,2,1,0:T(8,128)(2,1)} %fac_hbm.1), custom_call_target="tpu_custom_call" | custom-call | tf_op jit(solution)/shard_map/pallas_call | solution.py:470
  75.0 1.7 %shard_map.78 = (f32[4,32,256]{2,1,0:T(8,128)}, f32[4,32,256]{2,1,0:T(8,128)}) custom-call(f32[4,32,256]{2,1,0:T(8,128)} %get-tuple-element.4.a, f32[4,32,256]{2,1,0:T(8,128)} %get-tuple-element.5.b), custom_call_target="tpu_custom_call" | custom-call | tf_op jit(solution)/shard_map/pallas_call | solution.py:521
